TPU v7x, 32 devices: a whole 2x2x4 slice. The times are simulated.
32 devices in a mesh: grp: 4 (over y, x), tok: 8 (over z, core).
Axes of the slice: x: 2, y: 2, z: 4, core: 2. Of those that a mesh axis runs over, the one named last changes fastest.
Arguments:
- tokens: float32 [32768, 768], P(('grp', 'tok')), may hold values from -6 to 6
- cotangent: float32 [32768, 768], P(('grp', 'tok')), may hold values from -6 to 6
- crop_lengths: int32 [32, 10], P(('grp', 'tok')), may hold values from 54 to 261, as said below
- master: float32 [7088640], P('tok')
- first_moment: float32 [4, 7088640], P('grp', 'tok')
- second_moment: float32 [4, 7088640], P('grp', 'tok')
- outer_momentum: float32 [7088640], P('tok'), may hold values from -0.4375 to 0.4375
Outputs:
- block_output: float32 [32768, 768], P(('grp', 'tok'))
- input_grad: float32 [32768, 768], P(('grp', 'tok'))
- clip_norm: float32 [4], P('grp')
- vector_grads: float32 [4, 10752], P('grp', 'tok')
- first_moment_new: float32 [4, 7088640], P('grp', 'tok')
- second_moment_new: float32 [4, 7088640], P('grp', 'tok')
- mean_difference: float32 [7088640], P('tok')
- outer_momentum_new: float32 [7088640], P('tok')
- new_weights: float32 [7088640], P('tok')
Inputs may be any that keep to these rules, and one draw needn't show every extreme that they name: `crop_lengths`: each row holds, for each of its 1 images, 261 * 2 times and 54 * 8 times, in a drawn order.
All inputs are finite; a program needn't handle non-finite values.
Results may differ from a plain program's by a relative error of at most 0.012.
The roundings to bfloat16 on the way count: a program that leaves them out, or rounds other values in their place, can miss the bound.
Values may be sent and summed in bfloat16 or wider, within the bound.
A program may use at most 256 MiB of HBM per device.

v0:
```python
import jax
import jax.numpy as jnp
from jax import lax
from jax.sharding import PartitionSpec as P

D = 768
HEADS = 12
HEAD_DIM = 64
MLP = 3072


clip_limit = 3.0
beta_first = 0.9
beta_second = 0.999
adam_epsilon = 1e-08
weight_decay = 0.04
adam_count = 10.0
base_rate = 0.075
rate_scale = 0.9**6
outer_rate = 0.7
outer_beta = 0.9
norm_epsilon = 1e-06


def member_extents():
    return [(D, 3 * D), (D, D), (D, MLP), (MLP, D)] + [(D,)] * 8 + [(MLP,), (D,), (D,)]


def member_sizes():
    sizes_list = []
    for extent in member_extents():
        length = 1
        for member in extent:
            length = length * member
        sizes_list.append(length)
    return sizes_list


def split_params(flat_params, owners):
    table = flat_params.reshape(owners, -1)
    members = []
    offset = 0
    for extent, length in zip(member_extents(), member_sizes()):
        width = length // owners
        members.append(table[:, offset : offset + width].reshape(extent))
        offset = offset + width
    return members


def join_table(members, owners):
    return jnp.concatenate([member.reshape(owners, -1) for member in members], axis=1)


def layer_norm(values, norm_gain, norm_shift):
    center = values - jnp.mean(values, axis=-1, keepdims=True)
    spread = jnp.mean(center * center, axis=-1, keepdims=True)
    return center * lax.rsqrt(spread + norm_epsilon) * norm_gain + norm_shift


def pack_layout(lengths_row, row_count):
    ends_at = jnp.cumsum(lengths_row)
    position = jnp.arange(row_count, dtype=jnp.int32)
    segment = jnp.sum((position[:, None] >= ends_at[None, :]).astype(jnp.int32), axis=1)
    validity = (position < ends_at[-1]).astype(jnp.float32)
    return (segment, validity)


def cross_rows(left_side, right_side):
    return lax.dot_general(
        left_side, right_side, (((0,), (0,)), ((), ())), preferred_element_type=jnp.float32
    )


def times_transposed(left_side, right_side):
    return lax.dot_general(
        left_side, right_side, (((1,), (1,)), ((), ())), preferred_element_type=jnp.float32
    )


def on_device(tokens, cotangent, crop_lengths, master, first_moment, second_moment, outer_momentum):
    row_count = tokens.shape[0]
    pair_count = HEADS // 2
    score_scale = HEAD_DIM ** (-0.5)
    owners = lax.axis_size("tok")
    segment, validity = pack_layout(crop_lengths[0], row_count)
    allowed = segment[:, None] == segment[None, :]
    master_low = master.astype(jnp.bfloat16)
    gathered = split_params(lax.all_gather(master_low, "tok", axis=0, tiled=True), owners)
    w_qkv, w_proj, w_fc1, w_fc2 = gathered[:4]
    (
        gain_one,
        shift_one,
        query_bias,
        value_bias,
        proj_bias,
        scale_one,
        gain_two,
        shift_two,
        fc1_bias,
        fc2_bias,
        scale_two,
    ) = [member.astype(jnp.float32) for member in gathered[4:]]

    def to_pairs(block_cols):
        return jnp.moveaxis(block_cols.reshape(row_count, pair_count, 2 * HEAD_DIM), 1, 0)

    def from_pairs(paired):
        return jnp.moveaxis(paired, 0, 1).reshape(row_count, D)

    normed = layer_norm(tokens, gain_one, shift_one).astype(jnp.bfloat16)
    qkv_bias = jnp.concatenate([query_bias, jnp.zeros_like(query_bias), value_bias])
    projected = (jnp.dot(normed, w_qkv, preferred_element_type=jnp.float32) + qkv_bias).astype(
        jnp.bfloat16
    )
    query_pairs = to_pairs(projected[:, :D])
    key_pairs = to_pairs(projected[:, D : 2 * D])
    value_pairs = to_pairs(projected[:, 2 * D :])

    def forward_pair(pair_item):
        queries, keys_pair, values_pair = [
            member.reshape(row_count, 2, HEAD_DIM) for member in pair_item
        ]
        raw_scores = jnp.einsum(
            "qhd,khd->hqk", queries, keys_pair, preferred_element_type=jnp.float32
        )
        scores = jnp.where(allowed[None], raw_scores * score_scale, -1e30)
        largest = jnp.max(scores, axis=-1, keepdims=True)
        weights_exp = jnp.exp(scores - largest)
        totals = jnp.sum(weights_exp, axis=-1, keepdims=True)
        weights_low = (weights_exp / totals).astype(jnp.bfloat16)
        attended_pair = jnp.einsum(
            "hqk,khd->qhd", weights_low, values_pair, preferred_element_type=jnp.float32
        )
        return (attended_pair.reshape(row_count, 2 * HEAD_DIM), (largest + jnp.log(totals))[..., 0])

    attended_pairs, log_totals = lax.map(forward_pair, (query_pairs, key_pairs, value_pairs))
    attended = from_pairs(attended_pairs).astype(jnp.bfloat16)
    branch_one = jnp.dot(attended, w_proj, preferred_element_type=jnp.float32) + proj_bias
    middle = tokens + scale_one * branch_one
    normed_two = layer_norm(middle, gain_two, shift_two).astype(jnp.bfloat16)
    hidden_pre = jnp.dot(normed_two, w_fc1, preferred_element_type=jnp.float32) + fc1_bias
    hidden = jax.nn.gelu(hidden_pre, approximate=False).astype(jnp.bfloat16)
    branch_two = jnp.dot(hidden, w_fc2, preferred_element_type=jnp.float32) + fc2_bias
    block_output = middle + scale_two * branch_two
    back_out = cotangent * validity[:, None]
    grad_branch_two = (scale_two * back_out).astype(jnp.bfloat16)
    grad_scale_two = jnp.sum(back_out * branch_two, axis=0)
    grad_fc2_bias = jnp.sum(grad_branch_two.astype(jnp.float32), axis=0)
    grad_w_fc2 = cross_rows(hidden, grad_branch_two)
    grad_hidden = times_transposed(grad_branch_two, w_fc2)
    gelu_pull = jax.vjp(lambda values: jax.nn.gelu(values, approximate=False), hidden_pre)[1]
    grad_pre = gelu_pull(grad_hidden)[0].astype(jnp.bfloat16)
    grad_fc1_bias = jnp.sum(grad_pre.astype(jnp.float32), axis=0)
    grad_w_fc1 = cross_rows(normed_two, grad_pre)
    grad_normed_two = times_transposed(grad_pre, w_fc1)
    norm_pull = jax.vjp(layer_norm, middle, gain_two, shift_two)[1]
    grad_middle_part, grad_gain_two, grad_shift_two = norm_pull(grad_normed_two)
    grad_middle = back_out + grad_middle_part
    grad_scale_one = jnp.sum(grad_middle * branch_one, axis=0)
    grad_branch_one = (scale_one * grad_middle).astype(jnp.bfloat16)
    grad_proj_bias = jnp.sum(grad_branch_one.astype(jnp.float32), axis=0)
    grad_w_proj = cross_rows(attended, grad_branch_one)
    grad_attended = times_transposed(grad_branch_one, w_proj).astype(jnp.bfloat16)

    def backward_pair(pair_item):
        queries, keys_pair, values_pair, grad_pair = [
            member.reshape(row_count, 2, HEAD_DIM) for member in pair_item[:4]
        ]
        log_total = pair_item[4]
        raw_scores = jnp.einsum(
            "qhd,khd->hqk", queries, keys_pair, preferred_element_type=jnp.float32
        )
        scores = jnp.where(allowed[None], raw_scores * score_scale, -1e30)
        weights_soft = jnp.exp(scores - log_total[..., None])
        grad_values = jnp.einsum(
            "hqk,qhd->khd",
            weights_soft.astype(jnp.bfloat16),
            grad_pair,
            preferred_element_type=jnp.float32,
        )
        grad_weights = jnp.einsum(
            "qhd,khd->hqk", grad_pair, values_pair, preferred_element_type=jnp.float32
        )
        row_dot = jnp.sum(weights_soft * grad_weights, axis=-1, keepdims=True)
        grad_scores = (weights_soft * (grad_weights - row_dot)).astype(jnp.bfloat16)
        grad_queries = (
            jnp.einsum("hqk,khd->qhd", grad_scores, keys_pair, preferred_element_type=jnp.float32)
            * score_scale
        )
        grad_keys = (
            jnp.einsum("hqk,qhd->khd", grad_scores, queries, preferred_element_type=jnp.float32)
            * score_scale
        )
        return (
            grad_queries.reshape(row_count, 2 * HEAD_DIM),
            grad_keys.reshape(row_count, 2 * HEAD_DIM),
            grad_values.reshape(row_count, 2 * HEAD_DIM),
        )

    grad_q_pairs, grad_k_pairs, grad_v_pairs = lax.map(
        backward_pair, (query_pairs, key_pairs, value_pairs, to_pairs(grad_attended), log_totals)
    )
    grad_projected = jnp.concatenate(
        [from_pairs(grad_q_pairs), from_pairs(grad_k_pairs), from_pairs(grad_v_pairs)], axis=1
    ).astype(jnp.bfloat16)
    grad_query_bias = jnp.sum(grad_projected[:, :D].astype(jnp.float32), axis=0)
    grad_value_bias = jnp.sum(grad_projected[:, 2 * D :].astype(jnp.float32), axis=0)
    grad_w_qkv = cross_rows(normed, grad_projected)
    grad_normed = times_transposed(grad_projected, w_qkv)
    first_pull = jax.vjp(layer_norm, tokens, gain_one, shift_one)[1]
    grad_tokens_part, grad_gain_one, grad_shift_one = first_pull(grad_normed)
    input_grad = grad_middle + grad_tokens_part
    all_members = [
        grad_w_qkv,
        grad_w_proj,
        grad_w_fc1,
        grad_w_fc2,
        grad_gain_one,
        grad_shift_one,
        grad_query_bias,
        grad_value_bias,
        grad_proj_bias,
        grad_scale_one,
        grad_gain_two,
        grad_shift_two,
        grad_fc1_bias,
        grad_fc2_bias,
        grad_scale_two,
    ]
    received = lax.all_to_all(
        join_table(all_members, owners).astype(jnp.bfloat16),
        "tok",
        split_axis=0,
        concat_axis=0,
        tiled=True,
    ).astype(jnp.float32)
    summed = jnp.sum(received, axis=0)
    matrix_width = (4 * D * D + 2 * D * MLP) // owners
    vector_part = summed[matrix_width:] / (owners * row_count) ** 0.5
    square_total = lax.psum(jnp.sum(summed * summed), "tok")
    norm_value = jnp.sqrt(square_total)
    clipped = summed * (clip_limit / (norm_value + 1e-06))
    moment_one = beta_first * first_moment[0] + (1.0 - beta_first) * clipped
    moment_two = beta_second * second_moment[0] + (1.0 - beta_second) * clipped * clipped
    corrected_one = moment_one / (1.0 - beta_first**adam_count)
    corrected_two = moment_two / (1.0 - beta_second**adam_count)
    shard_size = master.shape[0]
    local_index = jnp.arange(shard_size, dtype=jnp.int32)
    decay_mask = (local_index < matrix_width).astype(jnp.float32)
    step_rate = base_rate * rate_scale
    updated = master - step_rate * (
        corrected_one / (jnp.sqrt(corrected_two) + adam_epsilon)
        + weight_decay * decay_mask * master
    )
    mean_difference = lax.psum((master - updated).astype(jnp.bfloat16), "grp").astype(
        jnp.float32
    ) / lax.axis_size("grp")
    outer_new = outer_beta * outer_momentum + mean_difference
    new_weights = master - outer_rate * (mean_difference + outer_beta * outer_new)
    return (
        block_output,
        input_grad,
        norm_value.reshape(1),
        vector_part[None],
        moment_one[None],
        moment_two[None],
        mean_difference,
        outer_new,
        new_weights,
    )


def solution(mesh):
    return jax.shard_map(
        on_device,
        mesh=mesh,
        in_specs=(
            P(("grp", "tok"), None),
            P(("grp", "tok"), None),
            P(("grp", "tok"), None),
            P("tok"),
            P("grp", "tok"),
            P("grp", "tok"),
            P("tok"),
        ),
        out_specs=(
            P(("grp", "tok"), None),
            P(("grp", "tok"), None),
            P("grp"),
            P("grp", "tok"),
            P("grp", "tok"),
            P("grp", "tok"),
            P("tok"),
            P("tok"),
            P("tok"),
        ),
        check_vma=False,
    )
```

profile of v0, /device:TPU:0, one launch (start us, length us, event | category | flops | bytes accessed | tf_op | source)
XLA Modules:
  0.0 1679.6 jit_solution(12442384563823971731)
XLA Ops:
  10.7 5.3 broadcast.272
  16.0 27.6 %dynamic-update-slice = bf16[7088640]{0:T(1024)(128)(2,1)} dynamic-update-slice(bf16[7088640]{0:T(1024)(128)(2,1)} %broadcast.272, bf16[886080]{0:T(1024)(128)(2,1)S(1)} %convert_element_type.194, u32[]{:T(128)} %bitcast) | dynamic-update-slice | bytes 3544324
  46.0 3.2 reduce_sum.212
  49.4 3.9 copy.113
  55.1 276.8 %all-reduce.6.cloned.1.call-done = bf16[7088640]{0:T(1024)(128)(2,1)} async-done(((bf16[7088640]{0:T(1024)(128)(2,1)}), bf16[7088640]{0:T(1024)(128)(2,1)}) %all-reduce.6.cloned.1.call-update) | async-done | bytes 14177296
  331.9 26.1 %reshape.558 = bf16[8,886080]{1,0:T(8,128)(2,1)} reshape(bf16[7088640]{0:T(1024)(128)(2,1)} %all-reduce.6.cloned.1.call-done) | data formatting | bytes 28354560 | tf_op jit(solution)/shard_map/reshape | solution.py:40
  359.3 3.4 slice.86
  365.7 8.5 fusion.42
  374.4 5.4 reshape.559
  380.1 6.4 add_convert_fusion.1
  397.9 65.0 %while.28 = (s32[]{:T(128)}, bf16[6,1024,128]{1,2,0:T(8,128)(2,1)}, f32[6,2,1024]{2,1,0:T(2,128)}, bf16[6,1024,128]{1,2,0:T(8,128)(2,1)}, bf16[6,1024,128]{1,2,0...) while((s32[]{:T(128)}, bf16[6,1024,128]{1,2,0:T(8,128)(2,1)}, ...), condition=%wide.region_7.8_spmd.clone, body=%wide.region_4.7_spmd.clone.sunk | while | flops 563083264 | bytes 32575596 | solution.py:136
  404.5 2.8 fusion.101
  415.3 2.8 fusion.101
  426.1 2.8 fusion.101
  436.9 2.8 fusion.101
  447.7 2.8 fusion.101
  458.4 2.8 fusion.101
  463.0 2.9 reshape.564
  465.9 6.6 reshape.565
  472.6 5.2 fusion.41
  479.9 6.7 reshape.566
  486.6 3.1 fusion.38
  489.7 38.1 %multiply_convert_fusion.1 = (bf16[1024,3072]{1,0:T(8,128)(2,1)}, f32[1024,3072]{1,0:T(8,128)}, f32[1024,3072]{1,0:T(8,128)}) fusion(f32[3072]{0:T(1024)S(1)} %reshape.583, bf16[768,3072]{1,0:T(8,128)(2,1)} %reshape.565, f32[1024,768]{0,1:T(8,128)S(1)} %copy-done.3, f32[768]{0:T(1024)S(1)} %reshape.582, f32[768]{0:T(1024)S(1)} %reshape.581, ...), kind=kOutput, calls=%fused_computation.39 | convolution fusion | flops 5043388416 | bytes 39348224 | tf_op jit(solution)/shard_map/dot_general | solution.py:141
  527.8 17.8 %fusion.46 = (bf16[3072]{0:T(1024)(128)(2,1)}, bf16[1024,3072]{1,0:T(8,128)(2,1)}) fusion(f32[1024,3072]{1,0:T(8,128)} %get-tuple-element.241, bf16[1024,768]{0,1:T(8,128)(2,1)S(1)} %get-tuple-element.235, bf16[3072,768]{1,0:T(8,128)(2,1)} %reshape.566, f32[1024,3072]{1,0:T(8,128)} %get-tuple-element.272, f32[3072]{0:T(1024)S(1)} %reshape.583), kind=kOutput, calls=%fused_computation.145 | convolution fusion | flops 4882166784 | bytes 37767168 | tf_op jit(solution)/shard_map/dot_general | solution.py:75
  545.7 10.3 fusion.45
  555.9 3.5 copy.114
  564.2 14.7 multiply_reduce_fusion.4
  585.3 109.6 %while.29 = (s32[]{:T(128)}, bf16[6,1024,128]{1,2,0:T(8,128)(2,1)S(1)}, bf16[6,1024,128]{1,2,0:T(8,128)(2,1)}, bf16[6,1024,128]{1,2,0:T(8,128)(2,1)S(1)}, bf16[6...) while((s32[]{:T(128)}, ...), condition=%wide.region_14.15_spmd.clone, body=%wide.region_12.14_spmd.clone.sunk | while | flops 1375205376 | bytes 73461904 | solution.py:200
  591.9 3.4 multiply_reduce_fusion.13
  595.3 2.7 multiply_convert_fusion.7
  610.1 3.4 multiply_reduce_fusion.13
  628.4 3.4 multiply_reduce_fusion.13
  646.6 3.4 multiply_reduce_fusion.13
  664.8 3.4 multiply_reduce_fusion.13
  683.1 3.4 multiply_reduce_fusion.13
  696.6 9.1 fusion.44
  705.8 5.9 convolution_convert_fusion.2
  714.2 7.1 convolution_convert_fusion.1
  721.4 7.1 convolution_convert_fusion
  728.9 3.5 copy.115
  736.5 7.2 concatenate.66
  743.8 9.6 constant_dynamic-update-slice_fusion.8
  753.4 5.6 concatenate.67
  759.0 9.0 concatenate.68
  768.1 8.1 concatenate.69
  777.0 5.6 constant_dynamic-update-slice_fusion.7
  782.6 12.9 constant_dynamic-update-slice_fusion.6
  795.6 11.1 constant_dynamic-update-slice_fusion.5
  816.9 2.9 dynamic-update-slice.10
  829.7 254.3 %reduce.17 = bf16[8,886080]{1,0:T(8,128)(2,1)} reduce(bf16[8,1,886080]{2,1,0:T(2,128)(2,1)} %dynamic-update-slice.15, bf16[]{:T(256)} %broadcast.377), dimensions={1}, to_apply=%dynamic-update-slice.15.reduce_sub_computation | reduce | bytes 28354562 | tf_op jit(solution)/shard_map/concatenate | solution.py:51
  1084.0 48.5 %reshape.601 = bf16[8,2,443040]{2,1,0:T(2,128)(2,1)} reshape(bf16[8,886080]{1,0:T(8,128)(2,1)} %reduce.17) | data formatting | bytes 28354560
  1132.4 5.6 all-to-all-start
  1138.1 41.5 %multiply_reduce_fusion.10 = (f32[886080]{0:T(1024)}, f32[886080]{0:T(1024)}) fusion(f32[1,886080]{1,0:T(1,128)} %param.16, f32[1,886080]{1,0:T(1,128)} %param.15), kind=kLoop, calls=%fused_computation.94 | loop fusion | flops 1772160 | bytes 14177280 | tf_op jit(solution)/shard_map/mul | solution.py:244
  1179.6 3.5 copy.133
  1183.1 5.4 add_add_fusion.2
  1188.5 257.5 %all-to-all-done = bf16[8,2,443040]{2,1,0:T(2,128)(2,1)} async-done(((bf16[8,2,443040]{2,1,0:T(2,128)(2,1)}), bf16[8,2,443040]{2,1,0:T(2,128)(2,1)}, u32[]{:S(2)}, u32[]{:S(2)}) %all-to-all-start) | async-done | bytes 14177312 | tf_op jit(solution)/shard_map/all_to_all | solution.py:230
  1446.0 51.1 %reshape.602 = bf16[8,1,886080]{2,1,0:T(2,128)(2,1)} reshape(bf16[8,2,443040]{2,1,0:T(2,128)(2,1)} %all-to-all-done) | data formatting | bytes 28354560
  1497.2 74.8 %convert_reduce_fusion = f32[886080]{0:T(1024)S(1)} fusion(bf16[8,1,886080]{2,1,0:T(2,128)(2,1)} %reshape.602), kind=kLoop, calls=%fused_computation.35 | loop fusion | flops 13291200 | bytes 17721600 | tf_op jit(solution)/shard_map/reduce_sum | solution.py:237
  1573.5 3.5 copy.134
  1577.0 15.3 psum.14
  1593.1 7.1 fusion.27
  1600.2 17.1 %fusion.28 = (f32[1,886080]{1,0:T(1,128)}, f32[1,886080]{1,0:T(1,128)}) fusion(f32[886080]{0:T(1024)} %get-tuple-element.233, f32[1,886080]{1,0:T(1,128)} %param.16, f32[1,886080]{1,0:T(1,128)} %param.15), kind=kLoop, calls=%fused_computation.75 | loop fusion | flops 6202560 | bytes 17721600 | tf_op jit(solution)/shard_map/add | solution.py:244
  1617.9 45.1 %all-reduce.4.cloned.1.call-done = bf16[886080]{0:T(1024)(128)(2,1)} async-done(((bf16[886080]{0:T(1024)(128)(2,1)}), bf16[886080]{0:T(1024)(128)(2,1)}) %all-reduce.4.cloned.1.call-update) | async-done | bytes 1772176 | tf_op jit(solution)/shard_map/psum | solution.py:255
  1663.0 8.4 multiply_subtract_fusion
  (305 shorter events, 202.0 us)
Async XLA Ops:
  7.2 2.3 copy-start.44
  7.2 324.7 %all-reduce.6.cloned.1.call-start = ((), (), s32[]{:S(2)}) async-start(), calls=%async_computation.2 | async-start | bytes 28356608
  43.6 5.7 copy-start.43
  46.0 426.7 %copy-start = (f32[1024,768]{0,1:T(8,128)}, f32[1024,768]{0,1:T(8,128)S(1)}, u32[]{:S(2)}) copy-start(f32[1024,768]{0,1:T(8,128)S(1)} %copy.111) | copy-start | bytes 9437188
  54.6 325.5 %copy-start.21 = (f32[1024]{0:T(1024)}, f32[1024]{0:T(1024)S(1)}, u32[]{:S(2)}) copy-start(f32[1024]{0:T(1024)S(1)} %broadcast_multiply_fusion.2) | copy-start | bytes 12292
  55.0 302.9 %copy-start.29 = (f32[1024]{0:T(1024)}, f32[1024]{0:T(1024)S(1)}, u32[]{:S(2)}) copy-start(f32[1024]{0:T(1024)S(1)} %multiply_reduce_fusion.9) | copy-start | bytes 12292
  55.1 325.0 %copy-start.27 = (f32[1024]{0:T(1024)}, f32[1024]{0:T(1024)S(1)}, u32[]{:S(2)}) copy-start(f32[1024]{0:T(1024)S(1)} %fusion.31) | copy-start | bytes 12292
  374.4 98.2 %copy-start.23 = (f32[768]{0:T(1024)}, f32[768]{0:T(1024)S(1)}, u32[]{:S(2)}) copy-start(f32[768]{0:T(1024)S(1)} %reshape.574) | copy-start | bytes 9220
  380.0 6.5 copy-start.36
  380.1 6.4 copy-start.25
  463.0 9.5 copy-start.14
  472.5 17.1 %copy-start.38 = (f32[768]{0:T(1024)}, f32[768]{0:T(1024)S(1)}, u32[]{:S(2)}) copy-start(f32[768]{0:T(1024)S(1)} %reshape.582) | copy-start | bytes 9220
  477.8 1.7 copy-start.2
  486.6 3.1 copy-start.3
  489.7 38.1 %copy-start.19 = (bf16[1024,768]{0,1:T(8,128)(2,1)}, bf16[1024,768]{0,1:T(8,128)(2,1)S(1)}, u32[]{:S(2)}) copy-start(bf16[1024,768]{0,1:T(8,128)(2,1)S(1)} %get-tuple-element.235) | copy-start | bytes 4718596
  559.5 2.8 copy-start.6
  562.0 2.1 copy-start.31
  564.2 14.7 copy-start.24
  578.9 4.7 copy-start.7
  578.9 2.1 copy-start.13
  579.9 3.6 copy-start.16
  583.6 1.7 copy-start.15
  694.9 1.1 copy-start.9
  694.9 1.7 copy-start.11
  696.5 9.2 copy-start.1
  696.5 9.2 copy-start.10
  696.6 9.2 copy-start.12
  696.6 9.2 copy-start.18
  696.6 9.2 copy-start.22
  696.6 9.2 copy-start.26
  696.6 9.2 copy-start.28
  696.6 9.2 copy-start.37
  696.6 17.6 %slice-start.3 = ((s8[6291456]{0:T(1024)(128)(4,1)}), s8[4194304]{0:T(1024)(128)(4,1)S(1)}, s32[]{:S(2)}) async-start(s8[6291456]{0:T(1024)(128)(4,1)} %bitcast.164), calls=%async_computation.6 | async-start | bytes 8388608
  705.8 5.9 copy-start.8
  705.8 5.9 copy-start.17
  705.8 8.4 slice-start.4
  711.7 2.5 copy-start.4
  711.7 2.5 copy-start.39
  711.7 9.6 slice-start.5
  714.2 7.1 copy-start.20
  714.2 7.1 slice-start.6
  732.5 2.5 copy-start.30
  732.5 2.8 copy-start.5
  768.0 8.4 copy-start.33
  768.0 8.5 copy-start.42
  768.0 8.6 copy-start.32
  768.0 8.7 copy-start.40
  768.0 8.8 copy-start.35
  768.0 8.8 copy-start.34
  768.0 8.9 copy-start.41
  777.0 18.5 %slice-start = ((s8[9437184]{0:T(1024)(128)(4,1)}), s8[1048576]{0:T(1024)(128)(4,1)S(1)}, s32[]{:S(2)}) async-start(s8[9437184]{0:T(1024)(128)(4,1)} %bitcast.139), calls=%async_computation.3 | async-start | bytes 2097152
  782.6 12.9 slice-start.1
  782.6 12.9 slice-start.2
  1132.4 313.6 %all-to-all-start = ((bf16[8,2,443040]{2,1,0:T(2,128)(2,1)}), bf16[8,2,443040]{2,1,0:T(2,128)(2,1)}, u32[]{:S(2)}, u32[]{:S(2)}) async-start(bf16[8,2,443040]{2,1,0:T(2,128)(2,1)} %reshape.601), calls=%async_computation | async-start | bytes 28360704 | tf_op jit(solution)/shard_map/all_to_all | solution.py:230
  1138.0 525.0 %all-reduce.4.cloned.1.call-start = ((), (), s32[]{:S(2)}) async-start(), calls=%async_computation.1 | async-start | bytes 3547136 | tf_op jit(solution)/shard_map/psum | solution.py:255
Sparse Core Ops, SparseCore 0:
  43.7 288.1 all-reduce.5
  1600.3 62.6 all-reduce.3
where the time goes:
time: 1690 us; the launch traced here: 1680 us
  waiting for transfers between devices  579 us (34%)
  other arithmetic  472 us (28%)
  local copies, waits for them, and re-layouts  377 us (22%)
  matrix products  212 us (13%)
  between operations  17.4 us (1%)
    unnamed x3, waiting for transfers between devices  277 us
    all_to_all x1, waiting for transfers between devices, on_device(): lax.all_to_all(join_table(all_members, owners).astype(jnp.bfloat16), 'tok...  257 us
    concatenate x1, other arithmetic, join_table(): jnp.concatenate([member.reshape(owners, -1) for member in members], axis=1)  254 us
    unnamed x127, local copies, waits for them, and re-layouts  211 us
    reduce_sum x1, other arithmetic, on_device(): summed = jnp.sum(received, axis=0)  74.8 us
    psum x1, waiting for transfers between devices, on_device(): lax.psum((master - updated).astype(jnp.bfloat16), 'grp').astype(jnp.float32)  45.1 us
    mul x1, other arithmetic, on_device(): beta_second * second_moment[0] + (1.0 - beta_second) * clipped * clipped  41.5 us
    dot_general x4, matrix products, times_transposed(): lax.dot_general(left_side, right_side, (((1,), (1,)), ((), ())), preferre...  39.7 us
  transfers between devices with their start and end apart: 3, of which 3 were waited for; matrix products, arithmetic and copies ran while one was open for 5% of the time, Pallas kernels for 0%

commit v1 on v0

--- a/solution.py
+++ b/solution.py
@@ -1,12 +1,17 @@
+import functools
+
 import jax
 import jax.numpy as jnp
 from jax import lax
+from jax.experimental import pallas as pl
+from jax.experimental.pallas import tpu as pltpu
+
 from jax.sharding import PartitionSpec as P
 
 D = 768
+MLP = 3072
 HEADS = 12
 HEAD_DIM = 64
-MLP = 3072
 
 
 clip_limit = 3.0
@@ -270,9 +275,733 @@
     )
 
 
+ROWS = D // 8
+ANY = pl.BlockSpec(memory_space=pl.ANY)
+DMA = pltpu.SemaphoreType.DMA
+MESH_ID = pl.DeviceIdType.MESH
+NZ = 4
+
+
+def place():
+    g = lax.axis_index("grp")
+    t = lax.axis_index("tok")
+    z, c = lax.div(t, 2), lax.rem(t, 2)
+    gx = g + 1 - 2 * lax.rem(g, 2)
+    gy = g + 2 - 4 * lax.div(g, 2)
+    return g, t, z, c, gx, gy
+
+
+def greet(targets, count):
+    barrier = pltpu.get_barrier_semaphore()
+    for target in targets:
+        pl.semaphore_signal(barrier, inc=1, device_id=target, device_id_type=MESH_ID)
+    pl.semaphore_wait(barrier, count)
+
+
+def remote(src, dst, send, recv, target):
+    return pltpu.make_async_remote_copy(
+        src_ref=src, dst_ref=dst, send_sem=send, recv_sem=recv,
+        device_id=target, device_id_type=MESH_ID,
+    )
+
+
+def rows_at(ref, start, count):
+    return ref.at[pl.ds(pl.multiple_of(start, 16), count), :]
+
+
+def weight_strip(w, ref, t):
+    return rows_at(ref, t * (384 if w == 2 else 96), 384 if w == 2 else 96)
+
+
+def weight_block(w, ref, t, q, half=None):
+    lead, count = (0, 96) if half is None else (48 * half, 48)
+    if w == 2:
+        return rows_at(ref, t * 384 + q * 96 + lead, count)
+    return ref.at[
+        pl.ds(pl.multiple_of(t * 96 + lead, 16), count),
+        pl.ds(pl.multiple_of(q * 768, 768), 768),
+    ]
+
+
+def piece_block(w, ref, q):
+    return weight_block(w, ref, 0, q)
+
+
+def gather_kernel(pa, pb, pc, pv, wa, wb, wc, wv, ls, zs, zr, xs, xr, ys, yr, ds, dr, cs, cr, vs, vr):
+    g, t, z, c, gx, gy = place()
+    pieces, fulls = (pa, pb, pc), (wa, wb, wc)
+    peers = [lax.rem(t + k, 8) for k in range(1, 8)]
+    greet([(g, p) for p in peers] + [(gx, t), (gy, t)], 9)
+    other = t + 1 - 2 * c
+
+    def z_copy(w, d, s):
+        step = 1 if d == 0 else -1
+        src_t = t - 2 * step * s
+        src = piece_block(w, pieces[w], g) if s == 0 else weight_block(w, fulls[w], src_t, g)
+        ok = (z - s >= 0) & (z + 1 < NZ) if d == 0 else (z + s < NZ) & (z - 1 >= 0)
+        return ok, remote(src, weight_block(w, fulls[w], src_t, g), zs.at[w, d, s], zr.at[w, d, s], (g, t + 2 * step))
+
+    def from_t(d, s):
+        return t - 2 * (s + 1) if d == 0 else t + 2 * (s + 1)
+
+    def here(d, s):
+        return z - s - 1 >= 0 if d == 0 else z + s + 1 < NZ
+
+    def z_wait(w, d, s):
+        blk = weight_block(w, fulls[w], from_t(d, s), g)
+        remote(blk, blk, zs.at[w, d, s], zr.at[w, d, s], (g, other)).wait_recv()
+
+    def side_copy(w, d, s, axis):
+        blk = weight_block(w, fulls[w], from_t(d, s), g)
+        sems = (xs, xr) if axis == 0 else (ys, yr)
+        return remote(blk, blk, sems[0].at[w, d, s], sems[1].at[w, d, s], (gx if axis == 0 else gy, t))
+
+    def side_wait(w, d, s, axis):
+        blk = weight_block(w, fulls[w], from_t(d, s), gx if axis == 0 else gy)
+        sems = (xs, xr) if axis == 0 else (ys, yr)
+        remote(blk, blk, sems[0].at[w, d, s], sems[1].at[w, d, s], (gx, t)).wait_recv()
+
+    def diag_copy(w, d, s, axis):
+        blk = weight_block(w, fulls[w], from_t(d, s), gx if axis == 0 else gy, axis)
+        return remote(blk, blk, ds.at[w, d, s, axis], dr.at[w, d, s, axis], (gy if axis == 0 else gx, t))
+
+    def diag_wait(w, d, s, axis):
+        blk = weight_block(w, fulls[w], from_t(d, s), 3 - g, axis)
+        remote(blk, blk, ds.at[w, d, s, axis], dr.at[w, d, s, axis], (gx, t)).wait_recv()
+
+    def core_copy(w, d, s):
+        blk = weight_strip(w, fulls[w], from_t(d, s))
+        return remote(blk, blk, cs.at[w, d, s], cr.at[w, d, s], (g, other))
+
+    def core_wait(w, d, s):
+        blk = weight_strip(w, fulls[w], from_t(d, s) + 1 - 2 * c)
+        remote(blk, blk, cs.at[w, d, s], cr.at[w, d, s], (g, other)).wait_recv()
+
+    def own_copy(w):
+        return remote(pieces[w], weight_strip(w, fulls[w], t), cs.at[w, 2, 0], cr.at[w, 2, 0], (g, other))
+
+    def both(s, fn):
+        for d in (0, 1):
+            @pl.when(here(d, s))
+            def _():
+                fn(d)
+
+    def start_z(w, s):
+        for d in (0, 1):
+            ok, copy = z_copy(w, d, s)
+
+            @pl.when(ok)
+            def _():
+                copy.start()
+
+    local_v = pltpu.make_async_copy(pv, wv.at[t], ls.at[3])
+    local_v.start()
+    v_copies = [remote(pv, wv.at[t], vs.at[k], vr.at[k], (g, peers[k])) for k in range(7)]
+    for copy in v_copies:
+        copy.start()
+    start_z(0, 0)
+    locals_ = [pltpu.make_async_copy(pieces[w], weight_strip(w, fulls[w], t), ls.at[w]) for w in range(3)]
+    for copy in locals_:
+        copy.start()
+    own_copy(0).start()
+
+    def arrive(w, s):
+        def fn(d):
+            z_wait(w, d, s)
+        both(s, fn)
+        if s < 2:
+            start_z(w, s + 1)
+
+        def sides(d):
+            side_copy(w, d, s, 0).start()
+            side_copy(w, d, s, 1).start()
+        both(s, sides)
+
+    def cross(w, s):
+        def fn(d):
+            for axis in (0, 1):
+                side_wait(w, d, s, axis)
+                diag_copy(w, d, s, axis).start()
+        both(s, fn)
+
+    def finish(w, s):
+        def fn(d):
+            diag_wait(w, d, s, 0)
+            diag_wait(w, d, s, 1)
+            core_copy(w, d, s).start()
+        both(s, fn)
+
+    for n in range(9):
+        w, s = divmod(n, 3)
+        arrive(w, s)
+        if s == 0 and w < 2:
+            start_z(w + 1, 0)
+            own_copy(w + 1).start()
+        if n >= 2:
+            cross((n - 2) // 3, (n - 2) % 3)
+        if n >= 3:
+            finish((n - 3) // 3, (n - 3) % 3)
+    cross(2, 1)
+    finish(2, 0)
+    cross(2, 2)
+    finish(2, 1)
+    finish(2, 2)
+    for k in range(7):
+        remote(pv, wv.at[lax.rem(t + 7 - k, 8)], vs.at[k], vr.at[k], (g, peers[k])).wait_recv()
+        v_copies[k].wait_send()
+    local_v.wait()
+    for w in range(3):
+        locals_[w].wait()
+        blk = weight_strip(w, fulls[w], other)
+        remote(pieces[w], blk, cs.at[w, 2, 0], cr.at[w, 2, 0], (g, other)).wait_recv()
+        own_copy(w).wait_send()
+        for s in range(3):
+            for d in (0, 1):
+                ok, copy = z_copy(w, d, s)
+
+                @pl.when(ok)
+                def _():
+                    copy.wait_send()
+
+            def fn(d):
+                core_wait(w, d, s)
+                side_copy(w, d, s, 0).wait_send()
+                side_copy(w, d, s, 1).wait_send()
+                diag_copy(w, d, s, 0).wait_send()
+                diag_copy(w, d, s, 1).wait_send()
+                core_copy(w, d, s).wait_send()
+            both(s, fn)
+
+
+def gather_weights(pa, pb, pc, pv):
+    return pl.pallas_call(
+        gather_kernel,
+        name="gather_weights",
+        out_shape=[
+            jax.ShapeDtypeStruct((D, 4 * D), jnp.bfloat16),
+            jax.ShapeDtypeStruct((D, MLP), jnp.bfloat16),
+            jax.ShapeDtypeStruct((MLP, D), jnp.bfloat16),
+            jax.ShapeDtypeStruct((8, 16, 128), jnp.float32),
+        ],
+        in_specs=[ANY] * 4,
+        out_specs=[ANY] * 4,
+        scratch_shapes=[
+            DMA((4,)),
+            DMA((3, 2, 3)), DMA((3, 2, 3)),
+            DMA((3, 2, 3)), DMA((3, 2, 3)),
+            DMA((3, 2, 3)), DMA((3, 2, 3)),
+            DMA((3, 2, 3, 2)), DMA((3, 2, 3, 2)),
+            DMA((3, 3, 3)), DMA((3, 3, 3)),
+            DMA((7,)), DMA((7,)),
+        ],
+        compiler_params=pltpu.CompilerParams(collective_id=0, has_side_effects=True),
+    )(pa, pb, pc, pv)
+
+
+def scatter_kernel(ga, gb, gc, gv, sa, sb, sc, sv, sq, own_ab, own_c, core_ab, core_c, z_ab, z_c, vbuf, qbuf, ls, cs, cr, zs, zr, vs, vr, qs, qr):
+    g, t, z, c, gx, gy = place()
+    peers = [lax.rem(t + k, 8) for k in range(1, 8)]
+    greet([(g, p) for p in peers], 7)
+    other = t + 1 - 2 * c
+    grads = (ga, gb, gc)
+    order = (2, 1, 0)
+    own = (own_ab.at[0], own_ab.at[1], own_c)
+    core = (core_ab.at[0], core_ab.at[1], core_c)
+    zbuf = (z_ab.at[0], z_ab.at[1], z_c)
+
+    def core_copy(w, k):
+        return remote(weight_strip(w, grads[w], 2 * k + 1 - c), core[w].at[k], cs.at[w, k], cr.at[w, k], (g, other))
+
+    def load(w, k):
+        return pltpu.make_async_copy(weight_strip(w, grads[w], 2 * k + c), own[w].at[k], ls.at[w, k])
+
+    v_copies = [remote(gv.at[peers[k]], vbuf.at[k], vs.at[k], vr.at[k], (g, peers[k])) for k in range(7)]
+    by_need = (3, 0, 2, 1)
+    for w in order:
+        for k in by_need:
+            core_copy(w, k).start()
+            load(w, k).start()
+        if w == 2:
+            for copy in v_copies:
+                copy.start()
+
+    def half_at(w, h):
+        n = 192 if w == 2 else 48
+        return pl.ds(h * n, n)
+
+    def add_rows(w, k, h, extra, out=None):
+        rows = 192 if w == 2 else 48
+        chunk = 64 if w == 2 else 16
+
+        def body(i, _):
+            at = pl.ds(pl.multiple_of(h * rows + i * chunk, chunk), chunk)
+            total = own[w][k, at, :].astype(jnp.float32) + core[w][k, at, :].astype(jnp.float32)
+            for d in extra:
+                total = total + zbuf[w][d, k, at, :].astype(jnp.float32)
+            if out is None:
+                own[w][k, at, :] = total.astype(jnp.bfloat16)
+            else:
+                out[at, :] = total
+            return 0
+        lax.fori_loop(0, rows // chunk, body, 0)
+
+    def z_copy(w, d, k, h):
+        step = 2 if d == 0 else -2
+        at = half_at(w, h)
+        return remote(
+            own[w].at[k, at, :], zbuf[w].at[d, k, at, :], zs.at[w, d, k, h], zr.at[w, d, k, h], (g, t + step)
+        )
+
+    def z_wait(w, d, k, h):
+        z_copy(w, d, k, h).wait_recv()
+
+    def ready(w, k):
+        load(w, k).wait()
+        core_copy(w, k).wait_recv()
+
+    def pass_on(i, d, j, h):
+        w = order[i]
+        reach = NZ - 1 - z if d == 0 else z
+        k = z + j if d == 0 else z - j
+        first = z == 0 if d == 0 else z == NZ - 1
+
+        @pl.when(j <= reach)
+        def _():
+            if h == 0:
+                ready(w, k)
+
+            @pl.when(first)
+            def _():
+                add_rows(w, k, h, ())
+
+            @pl.when(jnp.logical_not(first))
+            def _():
+                z_wait(w, d, k, h)
+                add_rows(w, k, h, (d,))
+
+            if i > 0:
+                @pl.when(j == reach)
+                def _():
+                    z_copy(order[i - 1], d, z + 1 if d == 0 else z - 1, h).wait_send()
+            if j < NZ - 1:
+                @pl.when(j < reach)
+                def _():
+                    z_copy(w, d, k + 1 if d == 0 else k - 1, h).wait_send()
+            z_copy(w, d, k, h).start()
+
+    outs = (sa, sb, sc)
+
+    def settle(w):
+        for k in range(NZ):
+            @pl.when(z == k)
+            def _():
+                ready(w, k)
+                dirs = [d for d in (0, 1) if not (d == 0 and k == 0) and not (d == 1 and k == NZ - 1)]
+                for h in (0, 1):
+                    for d in dirs:
+                        z_wait(w, d, k, h)
+                    add_rows(w, k, h, dirs, outs[w])
+
+    for i, w in enumerate(order):
+        for j in (3, 2, 1):
+            for h in (0, 1):
+                pass_on(i, 0, j, h)
+                pass_on(i, 1, j, h)
+        if i:
+            settle(order[i - 1])
+    settle(order[-1])
+    sv[...] = gv[t]
+    for k in range(7):
+        remote(gv.at[t], vbuf.at[k], vs.at[k], vr.at[k], (g, peers[k])).wait_recv()
+    for k in range(7):
+        sv[...] += vbuf[k]
+
+    def square(ref, rows):
+        def body(i, acc):
+            v = ref[pl.ds(pl.multiple_of(i * 8, 8), 8), :]
+            return acc + v * v
+        acc = lax.fori_loop(0, rows // 8, body, jnp.zeros((8, ref.shape[1]), jnp.float32))
+        return jnp.sum(acc)
+    total = square(sa, 96) + square(sb, 96) + square(sc, 384) + jnp.sum(sv[...] * sv[...])
+    qbuf[7] = jnp.full((8, 128), total, jnp.float32)
+    q_copies = [remote(qbuf.at[7], qbuf.at[k], qs.at[k], qr.at[k], (g, peers[k])) for k in range(7)]
+    for copy in q_copies:
+        copy.start()
+    for k in range(7):
+        q_copies[k].wait_recv()
+    acc = qbuf[7]
+    for k in range(7):
+        acc = acc + qbuf[k]
+    sq[...] = acc
+    for k in range(7):
+        q_copies[k].wait_send()
+        v_copies[k].wait_send()
+    for w in order:
+        for k in range(NZ):
+            core_copy(w, k).wait_send()
+    for h in (0, 1):
+        @pl.when(z < NZ - 1)
+        def _():
+            z_copy(order[-1], 0, z + 1, h).wait_send()
+
+        @pl.when(z > 0)
+        def _():
+            z_copy(order[-1], 1, z - 1, h).wait_send()
+
+
+def scatter_grads(ga, gb, gc, gv):
+    vm = pl.BlockSpec(memory_space=pltpu.VMEM)
+    return pl.pallas_call(
+        scatter_kernel,
+        name="scatter_grads",
+        out_shape=[
+            jax.ShapeDtypeStruct((ROWS, 4 * D), jnp.float32),
+            jax.ShapeDtypeStruct((ROWS, MLP), jnp.float32),
+            jax.ShapeDtypeStruct((4 * ROWS, D), jnp.float32),
+            jax.ShapeDtypeStruct((16, 128), jnp.float32),
+            jax.ShapeDtypeStruct((8, 128), jnp.float32),
+        ],
+        in_specs=[ANY] * 3 + [vm],
+        out_specs=[vm] * 5,
+        scratch_shapes=[
+            pltpu.VMEM((2, NZ, ROWS, MLP), jnp.bfloat16),
+            pltpu.VMEM((NZ, 4 * ROWS, D), jnp.bfloat16),
+            pltpu.VMEM((2, NZ, ROWS, MLP), jnp.bfloat16),
+            pltpu.VMEM((NZ, 4 * ROWS, D), jnp.bfloat16),
+            pltpu.VMEM((2, 2, NZ, ROWS, MLP), jnp.bfloat16),
+            pltpu.VMEM((2, NZ, 4 * ROWS, D), jnp.bfloat16),
+            pltpu.VMEM((7, 16, 128), jnp.float32),
+            pltpu.VMEM((8, 8, 128), jnp.float32),
+            DMA((3, NZ)), DMA((3, NZ)), DMA((3, NZ)),
+            DMA((3, 2, NZ, 2)), DMA((3, 2, NZ, 2)),
+            DMA((7,)), DMA((7,)), DMA((7,)), DMA((7,)),
+        ],
+        compiler_params=pltpu.CompilerParams(
+            collective_id=1, has_side_effects=True, vmem_limit_bytes=60 * 2**20
+        ),
+    )(ga, gb, gc, gv)
+
+
+SUM_ROWS = 7040
+SUM_H, SUM_Q, SUM_E = SUM_ROWS // 2, SUM_ROWS // 4, SUM_ROWS // 8
+
+
+def mean_kernel(diff, out, part, mid, buf, ss, rs):
+    g, t, z, c, gx, gy = place()
+    greet([(gx, t), (gy, t)], 2)
+    xi, yi = lax.rem(g, 2), lax.div(g, 2)
+    hop = [((gx, t), (gy, t)), ((gy, t), (gx, t))]
+    mine = [(xi, yi), (yi, xi)]
+
+    def copies(h):
+        a, b = mine[h]
+        base = h * SUM_H
+        sent = rows_at(diff, base + (1 - a) * SUM_Q, SUM_Q)
+        one = remote(sent, part.at[h], ss.at[h, 0], rs.at[h, 0], hop[h][0])
+        two = remote(rows_at(mid.at[h], (1 - b) * SUM_E, SUM_E), buf.at[h], ss.at[h, 1], rs.at[h, 1], hop[h][1])
+        done = rows_at(out, base + a * SUM_Q + b * SUM_E, SUM_E)
+        three = remote(done, done, ss.at[h, 2], rs.at[h, 2], hop[h][1])
+        whole = rows_at(out, base + a * SUM_Q, SUM_Q)
+        four = remote(whole, whole, ss.at[h, 3], rs.at[h, 3], hop[h][0])
+        return one, two, three, four
+
+    steps = [copies(0), copies(1)]
+    chunk = 80
+
+    def at(lo, i):
+        return pl.ds(pl.multiple_of(lo + i * chunk, 16), chunk)
+
+    for h in (0, 1):
+        steps[h][0].start()
+    for h in (0, 1):
+        a, b = mine[h]
+        steps[h][0].wait_recv()
+        lo, src = (1 - b) * SUM_E, h * SUM_H + a * SUM_Q + (1 - b) * SUM_E
+
+        def first(i, _):
+            total = diff[at(src, i), :].astype(jnp.float32) + part[h, at(lo, i), :].astype(jnp.float32)
+            mid[h, at(lo, i), :] = total.astype(jnp.bfloat16)
+            return 0
+        lax.fori_loop(0, SUM_E // chunk, first, 0)
+        steps[h][1].start()
+    for h in (0, 1):
+        a, b = mine[h]
+        steps[h][1].wait_recv()
+        lo, src = b * SUM_E, h * SUM_H + a * SUM_Q + b * SUM_E
+
+        def second(i, _):
+            total = diff[at(src, i), :].astype(jnp.float32) + part[h, at(lo, i), :].astype(jnp.float32)
+            total = total + buf[h, at(0, i), :].astype(jnp.float32)
+            out[at(src, i), :] = (total * 0.25).astype(jnp.bfloat16)
+            return 0
+        lax.fori_loop(0, SUM_E // chunk, second, 0)
+        steps[h][2].start()
+    for h in (0, 1):
+        a, b = mine[h]
+        other = rows_at(out, h * SUM_H + a * SUM_Q + (1 - b) * SUM_E, SUM_E)
+        remote(other, other, ss.at[h, 2], rs.at[h, 2], hop[h][1]).wait_recv()
+        steps[h][2].wait_send()
+        steps[h][3].start()
+    for h in (0, 1):
+        a, b = mine[h]
+        other = rows_at(out, h * SUM_H + (1 - a) * SUM_Q, SUM_Q)
+        remote(other, other, ss.at[h, 3], rs.at[h, 3], hop[h][0]).wait_recv()
+        steps[h][0].wait_send()
+        steps[h][1].wait_send()
+        steps[h][3].wait_send()
+
+
+def mean_groups(diff):
+    vm = pl.BlockSpec(memory_space=pltpu.VMEM)
+    return pl.pallas_call(
+        mean_kernel,
+        name="mean_groups",
+        out_shape=jax.ShapeDtypeStruct((SUM_ROWS, 128), jnp.bfloat16),
+        in_specs=[vm],
+        out_specs=vm,
+        scratch_shapes=[
+            pltpu.VMEM((2, SUM_Q, 128), jnp.bfloat16),
+            pltpu.VMEM((2, SUM_Q, 128), jnp.bfloat16),
+            pltpu.VMEM((2, SUM_E, 128), jnp.bfloat16),
+            DMA((2, 4)), DMA((2, 4)),
+        ],
+        compiler_params=pltpu.CompilerParams(collective_id=2, has_side_effects=True),
+    )(diff)
+
+
+MATRIX_WIDTH = (4 * D * D + 2 * D * MLP) // 8
+
+
+def vector_piece(flat):
+    return jnp.pad(flat.reshape(14, ROWS), ((0, 2), (0, 128 - ROWS)))
+
+
+def split_vectors(wv):
+    parts = wv[:, :14, :ROWS]
+    singles = [parts[:, j].reshape(-1) for j in (0, 1, 2, 3, 4, 5, 6, 7, 12, 13)]
+    return singles[:8] + [parts[:, 8:12].reshape(-1)] + singles[8:]
+
+
+def join_vectors(vectors):
+    rows = [v.reshape(8, -1, ROWS) for v in vectors]
+    return jnp.pad(jnp.concatenate(rows, axis=1), ((0, 0), (0, 2), (0, 128 - ROWS)))
+
+
+def own_pieces(master):
+    def piece(offset, rows, cols):
+        return master[offset : offset + rows * cols].reshape(rows, cols).astype(jnp.bfloat16)
+
+    size = ROWS * D
+    pa = jnp.concatenate([piece(0, ROWS, 3 * D), piece(3 * size, ROWS, D)], axis=1)
+    pb = piece(4 * size, ROWS, MLP)
+    pc = piece(8 * size, 4 * ROWS, D)
+    pv = vector_piece(master[MATRIX_WIDTH:].astype(jnp.bfloat16).astype(jnp.float32))
+    return pa, pb, pc, pv
+
+
+def flat_grads(sa, sb, sc, sv):
+    return jnp.concatenate(
+        [
+            sa[:, : 3 * D].reshape(-1),
+            sa[:, 3 * D :].reshape(-1),
+            sb.reshape(-1),
+            sc.reshape(-1),
+            sv[:14, :ROWS].reshape(-1),
+        ]
+    )
+
+
+def optimizer(summed, norm_value, master, first_moment, second_moment, outer_momentum):
+    clipped = summed * (clip_limit / (norm_value + 1e-06))
+    moment_one = beta_first * first_moment[0] + (1.0 - beta_first) * clipped
+    moment_two = beta_second * second_moment[0] + (1.0 - beta_second) * clipped * clipped
+    corrected_one = moment_one / (1.0 - beta_first**adam_count)
+    corrected_two = moment_two / (1.0 - beta_second**adam_count)
+    decay_mask = (jnp.arange(master.shape[0], dtype=jnp.int32) < MATRIX_WIDTH).astype(jnp.float32)
+    step_rate = base_rate * rate_scale
+    difference = step_rate * (
+        corrected_one / (jnp.sqrt(corrected_two) + adam_epsilon)
+        + weight_decay * decay_mask * master
+    )
+    low = jnp.pad(difference.astype(jnp.bfloat16), (0, SUM_ROWS * 128 - master.shape[0]))
+    mean_difference = mean_groups(low.reshape(SUM_ROWS, 128)).reshape(-1)[: master.shape[0]]
+    mean_difference = mean_difference.astype(jnp.float32)
+    outer_new = outer_beta * outer_momentum + mean_difference
+    new_weights = master - outer_rate * (mean_difference + outer_beta * outer_new)
+    return moment_one, moment_two, mean_difference, outer_new, new_weights
+
+
+def on_small_slice(tokens, cotangent, crop_lengths, master, first_moment, second_moment, outer_momentum):
+    row_count = tokens.shape[0]
+    pair_count = HEADS // 2
+    score_scale = HEAD_DIM ** (-0.5)
+    segment, validity = pack_layout(crop_lengths[0], row_count)
+    allowed = segment[:, None] == segment[None, :]
+    wa, w_fc1, w_fc2, wv = gather_weights(*own_pieces(master))
+    w_qkv, w_proj = wa[:, : 3 * D], wa[:, 3 * D :]
+    (
+        gain_one,
+        shift_one,
+        query_bias,
+        value_bias,
+        proj_bias,
+        scale_one,
+        gain_two,
+        shift_two,
+        fc1_bias,
+        fc2_bias,
+        scale_two,
+    ) = split_vectors(wv)
+    def to_pairs(block_cols):
+        return jnp.moveaxis(block_cols.reshape(row_count, pair_count, 2 * HEAD_DIM), 1, 0)
+
+    def from_pairs(paired):
+        return jnp.moveaxis(paired, 0, 1).reshape(row_count, D)
+
+    normed = layer_norm(tokens, gain_one, shift_one).astype(jnp.bfloat16)
+    qkv_bias = jnp.concatenate([query_bias, jnp.zeros_like(query_bias), value_bias])
+    projected = (jnp.dot(normed, w_qkv, preferred_element_type=jnp.float32) + qkv_bias).astype(
+        jnp.bfloat16
+    )
+    query_pairs = to_pairs(projected[:, :D])
+    key_pairs = to_pairs(projected[:, D : 2 * D])
+    value_pairs = to_pairs(projected[:, 2 * D :])
+
+    def forward_pair(pair_item):
+        queries, keys_pair, values_pair = [
+            member.reshape(row_count, 2, HEAD_DIM) for member in pair_item
+        ]
+        raw_scores = jnp.einsum(
+            "qhd,khd->hqk", queries, keys_pair, preferred_element_type=jnp.float32
+        )
+        scores = jnp.where(allowed[None], raw_scores * score_scale, -1e30)
+        largest = jnp.max(scores, axis=-1, keepdims=True)
+        weights_exp = jnp.exp(scores - largest)
+        totals = jnp.sum(weights_exp, axis=-1, keepdims=True)
+        weights_low = (weights_exp / totals).astype(jnp.bfloat16)
+        attended_pair = jnp.einsum(
+            "hqk,khd->qhd", weights_low, values_pair, preferred_element_type=jnp.float32
+        )
+        return (attended_pair.reshape(row_count, 2 * HEAD_DIM), (largest + jnp.log(totals))[..., 0])
+
+    attended_pairs, log_totals = lax.map(forward_pair, (query_pairs, key_pairs, value_pairs))
+    attended = from_pairs(attended_pairs).astype(jnp.bfloat16)
+    branch_one = jnp.dot(attended, w_proj, preferred_element_type=jnp.float32) + proj_bias
+    middle = tokens + scale_one * branch_one
+    normed_two = layer_norm(middle, gain_two, shift_two).astype(jnp.bfloat16)
+    hidden_pre = jnp.dot(normed_two, w_fc1, preferred_element_type=jnp.float32) + fc1_bias
+    hidden = jax.nn.gelu(hidden_pre, approximate=False).astype(jnp.bfloat16)
+    branch_two = jnp.dot(hidden, w_fc2, preferred_element_type=jnp.float32) + fc2_bias
+    block_output = middle + scale_two * branch_two
+    back_out = cotangent * validity[:, None]
+    grad_branch_two = (scale_two * back_out).astype(jnp.bfloat16)
+    grad_scale_two = jnp.sum(back_out * branch_two, axis=0)
+    grad_fc2_bias = jnp.sum(grad_branch_two.astype(jnp.float32), axis=0)
+    grad_w_fc2 = cross_rows(hidden, grad_branch_two)
+    grad_hidden = times_transposed(grad_branch_two, w_fc2)
+    gelu_pull = jax.vjp(lambda values: jax.nn.gelu(values, approximate=False), hidden_pre)[1]
+    grad_pre = gelu_pull(grad_hidden)[0].astype(jnp.bfloat16)
+    grad_fc1_bias = jnp.sum(grad_pre.astype(jnp.float32), axis=0)
+    grad_w_fc1 = cross_rows(normed_two, grad_pre)
+    grad_normed_two = times_transposed(grad_pre, w_fc1)
+    norm_pull = jax.vjp(layer_norm, middle, gain_two, shift_two)[1]
+    grad_middle_part, grad_gain_two, grad_shift_two = norm_pull(grad_normed_two)
+    grad_middle = back_out + grad_middle_part
+    grad_scale_one = jnp.sum(grad_middle * branch_one, axis=0)
+    grad_branch_one = (scale_one * grad_middle).astype(jnp.bfloat16)
+    grad_proj_bias = jnp.sum(grad_branch_one.astype(jnp.float32), axis=0)
+    grad_w_proj = cross_rows(attended, grad_branch_one)
+    grad_attended = times_transposed(grad_branch_one, w_proj).astype(jnp.bfloat16)
+
+    def backward_pair(pair_item):
+        queries, keys_pair, values_pair, grad_pair = [
+            member.reshape(row_count, 2, HEAD_DIM) for member in pair_item[:4]
+        ]
+        log_total = pair_item[4]
+        raw_scores = jnp.einsum(
+            "qhd,khd->hqk", queries, keys_pair, preferred_element_type=jnp.float32
+        )
+        scores = jnp.where(allowed[None], raw_scores * score_scale, -1e30)
+        weights_soft = jnp.exp(scores - log_total[..., None])
+        grad_values = jnp.einsum(
+            "hqk,qhd->khd",
+            weights_soft.astype(jnp.bfloat16),
+            grad_pair,
+            preferred_element_type=jnp.float32,
+        )
+        grad_weights = jnp.einsum(
+            "qhd,khd->hqk", grad_pair, values_pair, preferred_element_type=jnp.float32
+        )
+        row_dot = jnp.sum(weights_soft * grad_weights, axis=-1, keepdims=True)
+        grad_scores = (weights_soft * (grad_weights - row_dot)).astype(jnp.bfloat16)
+        grad_queries = (
+            jnp.einsum("hqk,khd->qhd", grad_scores, keys_pair, preferred_element_type=jnp.float32)
+            * score_scale
+        )
+        grad_keys = (
+            jnp.einsum("hqk,qhd->khd", grad_scores, queries, preferred_element_type=jnp.float32)
+            * score_scale
+        )
+        return (
+            grad_queries.reshape(row_count, 2 * HEAD_DIM),
+            grad_keys.reshape(row_count, 2 * HEAD_DIM),
+            grad_values.reshape(row_count, 2 * HEAD_DIM),
+        )
+
+    grad_q_pairs, grad_k_pairs, grad_v_pairs = lax.map(
+        backward_pair, (query_pairs, key_pairs, value_pairs, to_pairs(grad_attended), log_totals)
+    )
+    grad_projected = jnp.concatenate(
+        [from_pairs(grad_q_pairs), from_pairs(grad_k_pairs), from_pairs(grad_v_pairs)], axis=1
+    ).astype(jnp.bfloat16)
+    grad_query_bias = jnp.sum(grad_projected[:, :D].astype(jnp.float32), axis=0)
+    grad_value_bias = jnp.sum(grad_projected[:, 2 * D :].astype(jnp.float32), axis=0)
+    grad_w_qkv = cross_rows(normed, grad_projected)
+    grad_normed = times_transposed(grad_projected, w_qkv)
+    first_pull = jax.vjp(layer_norm, tokens, gain_one, shift_one)[1]
+    grad_tokens_part, grad_gain_one, grad_shift_one = first_pull(grad_normed)
+    input_grad = grad_middle + grad_tokens_part
+    ga = jnp.concatenate([grad_w_qkv, grad_w_proj], axis=1).astype(jnp.bfloat16)
+    sa, sb, sc, sv, sq = scatter_grads(
+        ga, grad_w_fc1.astype(jnp.bfloat16), grad_w_fc2.astype(jnp.bfloat16), join_vectors(
+            [
+                grad_gain_one,
+                grad_shift_one,
+                grad_query_bias,
+                grad_value_bias,
+                grad_proj_bias,
+                grad_scale_one,
+                grad_gain_two,
+                grad_shift_two,
+                grad_fc1_bias,
+                grad_fc2_bias,
+                grad_scale_two,
+            ]
+        )
+    )
+    summed = flat_grads(sa, sb, sc, sv)
+    norm_value = jnp.sqrt(sq[0, 0])
+    vector_part = summed[MATRIX_WIDTH:] / (8 * row_count) ** 0.5
+    moment_one, moment_two, mean_difference, outer_new, new_weights = optimizer(
+        summed, norm_value, master, first_moment, second_moment, outer_momentum
+    )
+    return (
+        block_output,
+        input_grad,
+        norm_value.reshape(1),
+        vector_part[None],
+        moment_one[None],
+        moment_two[None],
+        mean_difference,
+        outer_new,
+        new_weights,
+    )
+
+
 def solution(mesh):
+    small = mesh.shape["grp"] == 4 and mesh.shape["tok"] == 8
     return jax.shard_map(
-        on_device,
+        on_small_slice if small else on_device,
         mesh=mesh,
         in_specs=(
             P(("grp", "tok"), None),

time: 1690 us -> 733 us (0.43)
  waiting for transfers between devices: 579 us -> 0 us
  other arithmetic: 472 us -> 139 us
  local copies, waits for them, and re-layouts: 377 us -> 132 us
  Pallas kernels: 0 us -> 234 us
    unnamed x3 -> x0, waiting for transfers between devices: 277 us -> none
    all_to_all x1 -> x0, waiting for transfers between devices: 257 us -> none  [on_device(): lax.all_to_all(join_table(all_members, owners).astype(jnp.bfloat16), 'tok...]
    concatenate x2 -> x4, other arithmetic: 254 us -> 5.54 us  [the longest x1 3.05 us: on_small_slice(): ga = jnp.concatenate([grad_w_qkv, grad_w_proj], axis=1).astype(jnp.bfloat16)]
    pallas_call x0 -> x3, Pallas kernels: none -> 234 us  [the longest x1 129 us: scatter_grads(): pl.pallas_call(scatter_kernel, name='scatter_grads', out_shape=[jax.Shape...]
    unnamed x127 -> x123, local copies, waits for them, and re-layouts: 211 us -> 28.7 us
    reduce_sum x5 -> x3, other arithmetic: 80.9 us -> 2.58 us  [the longest x1 1.09 us: on_small_slice(): grad_fc2_bias = jnp.sum(grad_branch_two.astype(jnp.float32), axis=0)]
    psum x1 -> x0, waiting for transfers between devices: 45.1 us -> none  [on_device(): lax.psum((master - updated).astype(jnp.bfloat16), 'grp').astype(jnp.float32)]
    reshape x5 -> x17, local copies, waits for them, and re-layouts: 47.6 us -> 4.6 us  [the longest x1 2.15 us: flat_grads(): sa[:, :3 * D].reshape(-1)]
  transfers between devices with their start and end apart: 3 -> 0, of which waited for: 3 -> 0; matrix products, arithmetic and copies ran while one was open for 5% -> 0% of each run, Pallas kernels for 0% -> 0%
where the time goes in v1:
time: 733 us; the launch traced here: 724 us
  Pallas kernels  234 us (32%)
  matrix products  214 us (29%)
  other arithmetic  139 us (19%)
  local copies, waits for them, and re-layouts  132 us (18%)
    pallas_call x1, Pallas kernels, scatter_grads(): pl.pallas_call(scatter_kernel, name='scatter_grads', out_shape=[jax.Shape...  129 us
    pallas_call x1, Pallas kernels, gather_weights(): pl.pallas_call(gather_kernel, name='gather_weights', out_shape=[jax.Shape...  67.8 us
    mul x1, other arithmetic, optimizer(): moment_one = beta_first * first_moment[0] + (1.0 - beta_first) * clipped  56 us
    dot_general x4, matrix products, times_transposed(): lax.dot_general(left_side, right_side, (((1,), (1,)), ((), ())), preferre...  41.8 us
    dot_general x1, matrix products, on_small_slice(): jnp.dot(normed_two, w_fc1, preferred_element_type=jnp.float32) + fc1_bias  37.9 us
    pallas_call x1, Pallas kernels, mean_groups(): pl.pallas_call(mean_kernel, name='mean_groups', out_shape=jax.ShapeDtypeS...  36.7 us
    dynamic_slice x36, local copies, waits for them, and re-layouts, on_small_slice(): lax.map(forward_pair, (query_pairs, key_pairs, value_pairs))  35.6 us
    unnamed x123, local copies, waits for them, and re-layouts  28.7 us

profile of v1, /device:TPU:0, one launch (start us, length us, event | category | flops | bytes accessed | tf_op | source)
XLA Modules:
  0.0 723.9 jit_solution(18011147017299567996)
XLA Ops:
  0.6 2.4 copy.60
  3.0 3.3 convert.31
  9.5 2.3 convert_element_type.110
  13.7 2.3 fusion.45
  18.1 2.3 convert_element_type.113.pc
  21.8 67.8 %gather_weights.1 = (bf16[768,3072]{1,0:T(8,128)(2,1)}, bf16[768,3072]{1,0:T(8,128)(2,1)}, bf16[3072,768]{1,0:T(8,128)(2,1)}, f32[8,16,128]{2,1,0:T(8,128)}) custom-call(bf16[96,3072]{1,0:T(8,128)(2,1)} %pad_maximum_fusion.4.pa, bf16[96,3072]{1,0:T(8,128)(2,1)} %convert_element_type.112.pb, bf16[384,768]{1,0:T(8,128)(2,1)} %convert_element_type.113.pc, ...), custom_call_target="tpu_custom_call" | custom-call | tf_op jit(solution)/shard_map/gather_weights/pallas_call | solution.py:477
  95.2 6.4 add_convert_fusion.1
  101.6 2.3 fusion.44
  103.9 2.6 copy.57
  106.5 2.6 copy.58
  109.0 2.6 copy.59
  113.2 65.1 %while.28 = (s32[]{:T(128)}, bf16[6,1024,128]{1,2,0:T(8,128)(2,1)}, f32[6,2,1024]{2,1,0:T(2,128)}, bf16[6,1024,128]{1,2,0:T(8,128)(2,1)}, bf16[6,1024,128]{1,2,0...) while((s32[]{:T(128)}, bf16[6,1024,128]{1,2,0:T(8,128)(2,1)}, ...), condition=%wide.region_7.8_spmd.clone, body=%wide.region_4.7_spmd.clone.sunk | while | flops 563083264 | bytes 32575596 | solution.py:887
  120.3 2.8 fusion.100
  131.1 2.8 fusion.100
  141.8 2.8 fusion.100
  152.6 2.8 fusion.100
  163.4 2.8 fusion.100
  174.1 2.8 fusion.100
  178.3 6.1 fusion.43
  185.4 2.3 multiply_reduce_fusion.7
  187.7 37.9 %multiply_convert_fusion.1 = (bf16[1024,3072]{1,0:T(8,128)(2,1)}, f32[1024,3072]{1,0:T(8,128)}, f32[1024,3072]{1,0:T(8,128)}) fusion(f32[3072]{0:T(1024)S(1)} %add.164, bf16[768,3072]{1,0:T(8,128)(2,1)} %get-tuple-element.113, f32[1024,768]{0,1:T(8,128)} %get-tuple-element.251, f32[768]{0:T(1024)S(1)} %add.161, f32[768]{0:T(1024)S(1)} %mul.347, ...), kind=kOutput, calls=%fused_computation.39 | convolution fusion | flops 5043388416 | bytes 39348224 | tf_op jit(solution)/shard_map/dot_general | solution.py:892
  225.6 2.4 copy.62
  230.6 18.2 %convert_reduce_fusion = (f32[3072]{0:T(1024)}, bf16[1024,3072]{1,0:T(8,128)(2,1)}) fusion(f32[1024,3072]{1,0:T(8,128)} %get-tuple-element.249, bf16[1024,768]{0,1:T(8,128)(2,1)S(1)} %get-tuple-element.243, bf16[3072,768]{1,0:T(8,128)(2,1)} %get-tuple-element.114, f32[1024,3072]{1,0:T(8,128)} %get-tuple-element.278, f32[3072]{0:T(1024)S(1)} %add.164), kind=kOutput, calls=%fused_computation.37 | convolution fusion | flops 4885312512 | bytes 37773312 | tf_op jit(solution)/shard_map/dot_general | solution.py:80
  248.8 10.3 %fusion.49 = (f32[768]{0:T(1024)}, f32[1024,768]{1,0:T(8,128)}) fusion(bf16[1024,3072]{1,0:T(8,128)(2,1)} %get-tuple-element.284, bf16[768,3072]{1,0:T(8,128)(2,1)} %get-tuple-element.113), kind=kOutput, calls=%fused_computation.158 | convolution fusion | flops 4832623616 | bytes 14158848 | tf_op jit(solution)/shard_map/dot_general | solution.py:80
  259.1 3.7 copy.63
  262.8 2.5 multiply_reduce_fusion.6
  267.5 14.9 %multiply_reduce_fusion.3 = (f32[768]{0:T(1024)}, f32[1024,768]{0,1:T(8,128)}, f32[768]{0:T(1024)}, f32[1024,768]{0,1:T(8,128)}) fusion(f32[1024,768]{0,1:T(8,128)} %get-tuple-element.277, f32[768]{0:T(1024)S(1)} %add.156, f32[1024]{0:T(1024)S(1)} %negate_multiply_fusion.2, f32[1024]{0:T(1024)S(1)} %multiply_multiply_fusion.8, ...), kind=kOutput, calls=%fused_computation.78 | convolution fusion | flops 4845205504 | bytes 29923328 | tf_op jit(solution)/shard_map/dot_general | solution.py:894
  282.4 3.7 copy.68
  287.1 4.4 convolution_convert_fusion.3
  295.5 114.8 %while.29 = (s32[]{:T(128)}, bf16[6,1024,128]{1,2,0:T(8,128)(2,1)}, bf16[6,1024,128]{1,2,0:T(8,128)(2,1)}, bf16[6,1024,128]{1,2,0:T(8,128)(2,1)}, bf16[6,1024,12...) while((s32[]{:T(128)}, bf16[6,1024,128]{1,2,0:T(8,128)(2,1)}, ...), condition=%wide.region_14.15_spmd.clone, body=%wide.region_12.14_spmd.clone.sunk | while | flops 1375205376 | bytes 73461904 | solution.py:951
  302.5 3.4 multiply_reduce_fusion.12
  305.9 2.7 multiply_convert_fusion.8
  310.2 2.5 fusion.112
  321.5 3.4 multiply_reduce_fusion.12
  324.9 2.7 multiply_convert_fusion.8
  329.3 2.5 fusion.112
  340.6 3.4 multiply_reduce_fusion.12
  344.0 2.7 multiply_convert_fusion.8
  348.3 2.5 fusion.112
  359.6 3.4 multiply_reduce_fusion.12
  363.0 2.7 multiply_convert_fusion.8
  367.4 2.5 fusion.112
  378.7 3.4 multiply_reduce_fusion.12
  382.1 2.7 multiply_convert_fusion.8
  386.4 2.5 fusion.112
  397.8 3.4 multiply_reduce_fusion.12
  401.2 2.7 multiply_convert_fusion.8
  405.5 2.5 fusion.112
  410.3 9.0 %fusion.48 = (f32[768]{0:T(1024)S(1)}, f32[1024,768]{1,0:T(8,128)}) fusion(bf16[768,3072]{1,0:T(8,128)(2,1)} %get-tuple-element.111, bf16[1024,768]{0,1:T(8,128)(2,1)} %bitcast.172, bf16[1024,768]{0,1:T(8,128)(2,1)} %bitcast.181, bf16[1024,768]{0,1:T(8,128)(2,1)} %bitcast.170), kind=kOutput, calls=%fused_computation.157 | convolution fusion | flops 3638820096 | bytes 11406336 | tf_op jit(solution)/shard_map/dot_general | solution.py:80
  419.3 3.8 copy.64
  423.2 2.5 multiply_reduce_fusion.5
  427.7 2.7 add_add_fusion.2
  430.3 3.5 copy.69
  433.9 3.5 convolution_convert_fusion.4
  437.4 4.1 convolution_convert_fusion.2
  441.5 3.0 pad_maximum_fusion.1.ga
  444.6 7.2 convolution_convert_fusion.1.gb
  451.9 7.2 convolution_convert_fusion.gc
  461.2 129.5 %scatter_grads.1 = (f32[96,3072]{1,0:T(8,128)}, f32[96,3072]{1,0:T(8,128)}, f32[384,768]{1,0:T(8,128)}, f32[16,128]{1,0:T(8,128)}, f32[8,128]{1,0:T(8,128)}) custom-call(bf16[768,3072]{1,0:T(8,128)(2,1)} %pad_maximum_fusion.1.ga, bf16[768,3072]{1,0:T(8,128)(2,1)} %convolution_convert_fusion.1.gb, bf16[3072,768]{1,0:T(8,128)(2,1)} %convolution_convert_fusion.gc, ...), custom_call_target="tpu_custom_call" | custom-call | tf_op jit(solution)/shard_map/scatter_grads/pallas_call | solution.py:654
  592.6 2.3 fusion.47
  605.2 56.0 %multiply_reduce_fusion.10 = (f32[886080]{0:T(1024)}, f32[1,886080]{1,0:T(1,128)}, f32[1,886080]{1,0:T(1,128)}, f32[886080]{0:T(1024)}) fusion(f32[1,886080]{1,0:T(1,128)} %param.15, f32[1,886080]{1,0:T(1,128)} %get-tuple-element.275, f32[]{:T(128)} %bitcast.26, f32[1,886080]{1,0:T(1,128)} %param.16), kind=kLoop, calls=%fused_computation.99 | loop fusion | flops 7088640 | bytes 24810244 | tf_op jit(solution)/shard_map/mul | solution.py:816
  669.4 6.5 multiply_convert_fusion.2
  677.3 36.7 %mean_groups.1 = bf16[7040,128]{1,0:T(8,128)(2,1)} custom-call(bf16[7040,128]{1,0:T(8,128)(2,1)} %pad_bitcast_fusion.diff), custom_call_target="tpu_custom_call" | custom-call | tf_op jit(solution)/shard_map/mean_groups/pallas_call | solution.py:756
  713.9 8.4 %multiply_subtract_fusion = (f32[886080]{0:T(1024)}, f32[886080]{0:T(1024)}, f32[886080]{0:T(1024)}) fusion(f32[886080]{0:T(1024)} %param.14, f32[886080]{0:T(1024)} %param.17, bf16[901120]{0:T(1024)(128)(2,1)} %bitcast.164), kind=kLoop, calls=%fused_computation.69 | loop fusion | flops 6202560 | bytes 19493760 | tf_op jit(solution)/shard_map/sub | solution.py:830
  (299 shorter events, 161.3 us)
Async XLA Ops:
  3.0 175.3 %copy-start = (f32[1024,768]{0,1:T(8,128)}, f32[1024,768]{0,1:T(8,128)S(1)}, u32[]{:S(2)}) copy-start(f32[1024,768]{0,1:T(8,128)S(1)} %copy.60) | copy-start | bytes 9437188
  6.4 1.2 copy-start.9
  91.7 86.6 %copy-start.24 = (f32[768]{0:T(1024)}, f32[768]{0:T(1024)S(1)}, u32[]{:S(2)}) copy-start(f32[768]{0:T(1024)S(1)} %mul.333) | copy-start | bytes 9220
  92.0 9.6 %copy-start.39 = (f32[768]{0:T(1024)}, f32[768]{0:T(1024)S(1)}, u32[]{:S(2)}) copy-start(f32[768]{0:T(1024)S(1)} %add.151) | copy-start | bytes 9220
  92.0 9.5 %copy-start.26 = (f32[768]{0:T(1024)}, f32[768]{0:T(1024)S(1)}, u32[]{:S(2)}) copy-start(f32[768]{0:T(1024)S(1)} %mul.338) | copy-start | bytes 9220
  94.2 7.4 %copy-start.22 = (f32[1024]{0:T(1024)}, f32[1024]{0:T(1024)S(1)}, u32[]{:S(2)}) copy-start(f32[1024]{0:T(1024)S(1)} %broadcast_multiply_fusion.2) | copy-start | bytes 12292
  94.6 0.6 copy-start.30
  95.2 6.4 copy-start.28
  106.5 5.2 copy-start.48
  111.8 1.4 copy-start.46
  178.3 6.1 copy-start.16
  185.3 2.3 copy-start.42
  225.6 2.4 copy-start.47
  225.6 3.8 copy-start.36
  228.0 20.7 %copy-start.8 = (f32[1024,768]{0,1:T(8,128)}, f32[1024,768]{0,1:T(8,128)S(1)}, u32[]{:S(2)}) copy-start(f32[1024,768]{0,1:T(8,128)S(1)} %copy.62) | copy-start | bytes 9437188
  230.6 18.2 %copy-start.19 = (bf16[1024,768]{0,1:T(8,128)(2,1)}, bf16[1024,768]{0,1:T(8,128)(2,1)S(1)}, u32[]{:S(2)}) copy-start(bf16[1024,768]{0,1:T(8,128)(2,1)S(1)} %get-tuple-element.243) | copy-start | bytes 4718596
  259.1 3.7 copy-start.2
  262.8 2.8 copy-start.5
  265.3 2.1 copy-start.35
  282.4 3.7 copy-start.6
  282.4 3.7 copy-start.25
  287.1 4.4 copy-start.21
  291.5 4.0 copy-start.17
  419.3 3.9 copy-start.1
  419.3 3.9 copy-start.23
  419.3 3.9 copy-start.27
  423.1 2.6 copy-start.31
  423.1 2.8 copy-start.4
  423.2 2.8 copy-start.29
  425.7 2.0 copy-start.7
  433.9 3.5 copy-start.10
  433.9 3.5 copy-start.12
  433.9 3.5 copy-start.18
  433.9 3.5 copy-start.40
  433.9 10.7 %slice-start = ((s8[6291456]{0:T(1024)(128)(4,1)}), s8[4194304]{0:T(1024)(128)(4,1)S(1)}, s32[]{:S(2)}) async-start(s8[6291456]{0:T(1024)(128)(4,1)} %bitcast.189), calls=%async_computation | async-start | bytes 8388608
  437.4 7.2 slice-start.1
  441.5 3.1 copy-start.3
  441.5 3.1 copy-start.43
  441.5 10.3 %slice-start.2 = ((s8[6291456]{0:T(1024)(128)(4,1)}), s8[2097152]{0:T(1024)(128)(4,1)S(1)}, s32[]{:S(2)}) async-start(s8[6291456]{0:T(1024)(128)(4,1)} %bitcast.191), calls=%async_computation.2 | async-start | bytes 4194304
  444.6 7.2 copy-start.20
  444.6 7.2 slice-start.3
  451.8 7.4 %copy-start.11 = (bf16[6,1024,128]{1,2,0:T(8,128)(2,1)S(1)}, bf16[6,1024,128]{1,2,0:T(8,128)(2,1)}, u32[]{:S(2)}) copy-start(bf16[6,1024,128]{1,2,0:T(8,128)(2,1)} %get-tuple-element.116) | copy-start | bytes 4718596
  451.8 7.4 %copy-start.13 = (bf16[6,1024,128]{1,2,0:T(8,128)(2,1)S(1)}, bf16[6,1024,128]{1,2,0:T(8,128)(2,1)}, u32[]{:S(2)}) copy-start(bf16[6,1024,128]{1,2,0:T(8,128)(2,1)} %get-tuple-element.118) | copy-start | bytes 4718596
  451.8 8.1 %copy-start.34 = (f32[768]{0:T(1024)S(1)}, f32[768]{0:T(1024)}, u32[]{:S(2)}) copy-start(f32[768]{0:T(1024)} %get-tuple-element.246) | copy-start | bytes 9220
  451.8 8.2 %copy-start.45 = (f32[768]{0:T(1024)S(1)}, f32[768]{0:T(1024)}, u32[]{:S(2)}) copy-start(f32[768]{0:T(1024)} %get-tuple-element.244) | copy-start | bytes 9220
  451.8 8.2 %copy-start.33 = (f32[768]{0:T(1024)S(1)}, f32[768]{0:T(1024)}, u32[]{:S(2)}) copy-start(f32[768]{0:T(1024)} %get-tuple-element.191) | copy-start | bytes 9220
  451.9 8.3 %copy-start.41 = (f32[768]{0:T(1024)S(1)}, f32[768]{0:T(1024)}, u32[]{:S(2)}) copy-start(f32[768]{0:T(1024)} %get-tuple-element.281) | copy-start | bytes 9220
  451.9 8.4 %copy-start.38 = (f32[3072]{0:T(1024)S(1)}, f32[3072]{0:T(1024)}, u32[]{:S(2)}) copy-start(f32[3072]{0:T(1024)} %get-tuple-element.283) | copy-start | bytes 36868
  451.9 8.5 %copy-start.37 = (f32[768]{0:T(1024)S(1)}, f32[768]{0:T(1024)}, u32[]{:S(2)}) copy-start(f32[768]{0:T(1024)} %get-tuple-element.242) | copy-start | bytes 9220
  451.9 8.5 %copy-start.44 = (f32[768]{0:T(1024)S(1)}, f32[768]{0:T(1024)}, u32[]{:S(2)}) copy-start(f32[768]{0:T(1024)} %get-tuple-element.267) | copy-start | bytes 9220
  592.6 6.3 copy-start.15
  596.8 5.0 copy-start.14
  600.1 4.4 copy-start.32
